TPU v7x, 32 devices: a whole 2x2x4 slice. The times are simulated.
32 devices in a mesh: dp: 8 (over z, y), fsdp: 4 (over x, core).
Axes of the slice: x: 2, y: 2, z: 4, core: 2. Of those that a mesh axis runs over, the one named last changes fastest.
Arguments:
- tokens: bfloat16 [32768, 1024], P(('dp', 'fsdp')), may hold values from -6 to 6
- lengths: int32 [32, 4], P(('dp', 'fsdp')), may hold values from 0 to 512, as said below
- cotangent: bfloat16 [32768, 1024], P(('dp', 'fsdp')), may hold values from -6 to 6
- query_weight: bfloat16 [1024, 1024], P(('dp', 'fsdp')), may hold values from -0.1875 to 0.1875
- key_weight: bfloat16 [1024, 1024], P(('dp', 'fsdp')), may hold values from -0.1875 to 0.1875
- value_weight: bfloat16 [1024, 1024], P(('dp', 'fsdp')), may hold values from -0.1875 to 0.1875
- mixer_weight: bfloat16 [1024, 1024], P(('dp', 'fsdp')), may hold values from -1.5 to 1.5
- query_bias: bfloat16 [1024], P(('dp', 'fsdp')), may hold values from -3 to 3
- value_bias: bfloat16 [1024], P(('dp', 'fsdp')), may hold values from -3 to 3
- mixer_bias: bfloat16 [1024], P(('dp', 'fsdp')), may hold values from -3 to 3
- attn_gain: bfloat16 [1024], P(('dp', 'fsdp')), may hold values from 0.099609375 to 1.8984375
- attn_shift: bfloat16 [1024], P(('dp', 'fsdp')), may hold values from -3 to 3
- inner_weight: bfloat16 [1024, 4096], P(('dp', 'fsdp')), may hold values from -0.1875 to 0.1875
- inner_bias: bfloat16 [4096], P(('dp', 'fsdp')), may hold values from -3 to 3
- outer_weight: bfloat16 [4096, 1024], P(('dp', 'fsdp')), may hold values from -0.125 to 0.125
- outer_bias: bfloat16 [1024], P(('dp', 'fsdp')), may hold values from -3 to 3
- final_gain: bfloat16 [1024], P(('dp', 'fsdp')), may hold values from 0.099609375 to 1.8984375
- final_shift: bfloat16 [1024], P(('dp', 'fsdp')), may hold values from -3 to 3
Outputs:
- layer_out: bfloat16 [32768, 1024], P(('dp', 'fsdp'))
- tokens_grad: float32 [32768, 1024], P(('dp', 'fsdp'))
- query_weight_grad: float32 [1024, 1024], P(('dp', 'fsdp'))
- key_weight_grad: float32 [1024, 1024], P(('dp', 'fsdp'))
- value_weight_grad: float32 [1024, 1024], P(('dp', 'fsdp'))
- mixer_weight_grad: float32 [1024, 1024], P(('dp', 'fsdp'))
- query_bias_grad: float32 [1024], P(('dp', 'fsdp'))
- value_bias_grad: float32 [1024], P(('dp', 'fsdp'))
- mixer_bias_grad: float32 [1024], P(('dp', 'fsdp'))
- attn_gain_grad: float32 [1024], P(('dp', 'fsdp'))
- attn_shift_grad: float32 [1024], P(('dp', 'fsdp'))
- inner_weight_grad: float32 [1024, 4096], P(('dp', 'fsdp'))
- inner_bias_grad: float32 [4096], P(('dp', 'fsdp'))
- outer_weight_grad: float32 [4096, 1024], P(('dp', 'fsdp'))
- outer_bias_grad: float32 [1024], P(('dp', 'fsdp'))
- final_gain_grad: float32 [1024], P(('dp', 'fsdp'))
- final_shift_grad: float32 [1024], P(('dp', 'fsdp'))
Inputs may be any that keep to these rules, and one draw needn't show every extreme that they name: Each device's lengths sum to at most 1024; its first length is 128 or more; a zero length is followed only by zeros; some device holds a sequence of exactly 512.
All inputs are finite; a program needn't handle non-finite values.
Results may differ from a plain program's by a relative error of at most 0.014.
Values may be sent and summed in bfloat16 or wider, within the bound.
A program may use at most 256 MiB of HBM per device.

v0:
```python
import jax
import jax.numpy as jnp
from jax import lax
from jax.sharding import PartitionSpec as P

HEAD_DIM = 64


EPS = 1e-06
NEG = -1e30


def slot_layout(lengths, num_rows):
    bounds = jnp.cumsum(lengths, axis=-1)
    position = jnp.arange(num_rows, dtype=jnp.int32)
    segment = jnp.sum((position[:, None] >= bounds[..., None, :]).astype(jnp.int32), axis=-1)
    usable = position < bounds[..., -1:]
    return (segment, usable)


def norm_forward(values_in, gain_vec, shift_vec):
    average = jnp.mean(values_in, axis=-1, keepdims=True)
    centred = values_in - average
    inv_std = lax.rsqrt(jnp.mean(centred * centred, axis=-1, keepdims=True) + EPS)
    normed = centred * inv_std
    return (normed * gain_vec.astype(jnp.float32) + shift_vec.astype(jnp.float32), normed, inv_std)


def norm_back(incoming, normed, inv_std, gain_vec):
    scaled = incoming * gain_vec.astype(jnp.float32)
    first_mean = jnp.mean(scaled, axis=-1, keepdims=True)
    second_mean = jnp.mean(scaled * normed, axis=-1, keepdims=True)
    values_grad = inv_std * (scaled - first_mean - normed * second_mean)
    return (values_grad, jnp.sum(incoming * normed, axis=0), jnp.sum(incoming, axis=0))


def gelu_slope(inner):
    return 0.5 * (1.0 + lax.erf(inner * 2.0 ** (-0.5))) + inner * jnp.exp(-0.5 * inner * inner) * (
        2.0 * jnp.pi
    ) ** (-0.5)


def masked_scores(query_block, key_rows, segment, usable, first_row):
    num_rows = query_block.shape[0]
    num_keys = key_rows.shape[0]
    scores = jnp.einsum(
        "qhd,khd->hqk", query_block, key_rows, preferred_element_type=jnp.float32
    ) * HEAD_DIM ** (-0.5)
    row_segment = lax.dynamic_slice_in_dim(segment, first_row, num_rows)
    row_place = first_row + jnp.arange(num_rows, dtype=jnp.int32)
    column = jnp.arange(num_keys, dtype=jnp.int32)
    allowed = (row_segment[:, None] == segment[None, :]) & usable[None, :] | (
        row_place[:, None] == column[None, :]
    )
    return jnp.where(allowed[None], scores, NEG)


def col_sum(array_in):
    return jnp.sum(array_in.astype(jnp.float32), axis=0)


def local(
    tokens,
    lengths,
    cotangent,
    query_weight,
    key_weight,
    value_weight,
    mixer_weight,
    query_bias,
    value_bias,
    mixer_bias,
    attn_gain,
    attn_shift,
    inner_weight,
    inner_bias,
    outer_weight,
    outer_bias,
    final_gain,
    final_shift,
):
    num_slots = tokens.shape[0]
    width = tokens.shape[1]
    num_heads = width // HEAD_DIM
    scale = HEAD_DIM ** (-0.5)
    block_rows = min(512, num_slots)
    num_blocks = num_slots // block_rows
    segment, usable = slot_layout(lengths, num_slots)
    segment = segment[0]
    usable = usable[0]
    f32 = jnp.float32
    bf16 = jnp.bfloat16
    (
        query_full,
        key_full,
        value_full,
        mixer_full,
        qbias_full,
        vbias_full,
        mbias_full,
        again_full,
        ashift_full,
    ) = (
        lax.all_gather(query_weight, ("dp", "fsdp"), axis=0, tiled=True),
        lax.all_gather(key_weight, ("dp", "fsdp"), axis=0, tiled=True),
        lax.all_gather(value_weight, ("dp", "fsdp"), axis=0, tiled=True),
        lax.all_gather(mixer_weight, ("dp", "fsdp"), axis=0, tiled=True),
        lax.all_gather(query_bias, ("dp", "fsdp"), axis=0, tiled=True),
        lax.all_gather(value_bias, ("dp", "fsdp"), axis=0, tiled=True),
        lax.all_gather(mixer_bias, ("dp", "fsdp"), axis=0, tiled=True),
        lax.all_gather(attn_gain, ("dp", "fsdp"), axis=0, tiled=True),
        lax.all_gather(attn_shift, ("dp", "fsdp"), axis=0, tiled=True),
    )
    inner_full, ibias_full, outer_full, obias_full, fgain_full, fshift_full = (
        lax.all_gather(inner_weight, ("dp", "fsdp"), axis=0, tiled=True),
        lax.all_gather(inner_bias, ("dp", "fsdp"), axis=0, tiled=True),
        lax.all_gather(outer_weight, ("dp", "fsdp"), axis=0, tiled=True),
        lax.all_gather(outer_bias, ("dp", "fsdp"), axis=0, tiled=True),
        lax.all_gather(final_gain, ("dp", "fsdp"), axis=0, tiled=True),
        lax.all_gather(final_shift, ("dp", "fsdp"), axis=0, tiled=True),
    )
    head_shape = (num_slots, num_heads, HEAD_DIM)
    queries = (
        (jnp.dot(tokens, query_full, preferred_element_type=f32) + qbias_full.astype(f32))
        .astype(bf16)
        .reshape(head_shape)
    )
    key_rows = (
        jnp.dot(tokens, key_full, preferred_element_type=f32).astype(bf16).reshape(head_shape)
    )
    value_rows = (
        (jnp.dot(tokens, value_full, preferred_element_type=f32) + vbias_full.astype(f32))
        .astype(bf16)
        .reshape(head_shape)
    )

    def attend_block(block_index):
        first_row = block_index * block_rows
        query_block = lax.dynamic_slice_in_dim(queries, first_row, block_rows, 0)
        scores = masked_scores(query_block, key_rows, segment, usable, first_row)
        largest = jnp.max(scores, axis=-1, keepdims=True)
        log_total = largest + jnp.log(jnp.sum(jnp.exp(scores - largest), axis=-1, keepdims=True))
        weights = jnp.exp(scores - log_total).astype(bf16)
        output = jnp.einsum("hqk,khd->qhd", weights, value_rows, preferred_element_type=f32).astype(
            bf16
        )
        return (output, log_total)

    attended, log_totals = lax.map(attend_block, jnp.arange(num_blocks, dtype=jnp.int32))
    attended = attended.reshape(num_slots, width)
    mixed = jnp.dot(attended, mixer_full, preferred_element_type=f32) + mbias_full.astype(f32)
    hidden, first_normed, first_inv = norm_forward(
        tokens.astype(f32) + mixed, again_full, ashift_full
    )
    hidden_low = hidden.astype(bf16)
    inner = jnp.dot(hidden_low, inner_full, preferred_element_type=f32) + ibias_full.astype(f32)
    activated = jax.nn.gelu(inner, approximate=False).astype(bf16)
    outer = jnp.dot(activated, outer_full, preferred_element_type=f32) + obias_full.astype(f32)
    final, second_normed, second_inv = norm_forward(hidden + outer, fgain_full, fshift_full)
    layer_out = final.astype(bf16)
    query_full, key_full, value_full, mixer_full = (
        lax.all_gather(query_weight, ("dp", "fsdp"), axis=0, tiled=True),
        lax.all_gather(key_weight, ("dp", "fsdp"), axis=0, tiled=True),
        lax.all_gather(value_weight, ("dp", "fsdp"), axis=0, tiled=True),
        lax.all_gather(mixer_weight, ("dp", "fsdp"), axis=0, tiled=True),
    )
    inner_full, outer_full = (
        lax.all_gather(inner_weight, ("dp", "fsdp"), axis=0, tiled=True),
        lax.all_gather(outer_weight, ("dp", "fsdp"), axis=0, tiled=True),
    )
    out_grad = cotangent.astype(f32) * usable[:, None].astype(f32)
    second_grad, fgain_grad, fshift_grad = norm_back(
        out_grad, second_normed, second_inv, fgain_full
    )
    outer_low = second_grad.astype(bf16)
    outer_wgrad = jnp.einsum("sf,sd->fd", activated, outer_low, preferred_element_type=f32)
    outer_bgrad = col_sum(outer_low)
    act_grad = jnp.einsum("sd,fd->sf", outer_low, outer_full, preferred_element_type=f32)
    inner_low = (act_grad * gelu_slope(inner)).astype(bf16)
    inner_wgrad = jnp.einsum("sd,sf->df", hidden_low, inner_low, preferred_element_type=f32)
    inner_bgrad = col_sum(inner_low)
    hidden_grad = second_grad + jnp.einsum(
        "sf,df->sd", inner_low, inner_full, preferred_element_type=f32
    )
    ffn_shares = (
        lax.psum_scatter(inner_wgrad, ("dp", "fsdp"), scatter_dimension=0, tiled=True),
        lax.psum_scatter(inner_bgrad, ("dp", "fsdp"), scatter_dimension=0, tiled=True),
        lax.psum_scatter(outer_wgrad, ("dp", "fsdp"), scatter_dimension=0, tiled=True),
        lax.psum_scatter(outer_bgrad, ("dp", "fsdp"), scatter_dimension=0, tiled=True),
        lax.psum_scatter(fgain_grad, ("dp", "fsdp"), scatter_dimension=0, tiled=True),
        lax.psum_scatter(fshift_grad, ("dp", "fsdp"), scatter_dimension=0, tiled=True),
    )
    first_grad, again_grad, ashift_grad = norm_back(
        hidden_grad, first_normed, first_inv, again_full
    )
    mixed_low = first_grad.astype(bf16)
    mixer_wgrad = jnp.einsum("sa,sd->ad", attended, mixed_low, preferred_element_type=f32)
    mixer_bgrad = col_sum(mixed_low)
    attended_grad = (
        jnp.einsum("sd,ad->sa", mixed_low, mixer_full, preferred_element_type=f32)
        .astype(bf16)
        .reshape(head_shape)
    )

    def back_block(carry, block_index):
        key_acc, value_acc = carry
        first_row = block_index * block_rows
        query_block = lax.dynamic_slice_in_dim(queries, first_row, block_rows, 0)
        grad_block = lax.dynamic_slice_in_dim(attended_grad, first_row, block_rows, 0)
        scores = masked_scores(query_block, key_rows, segment, usable, first_row)
        weights = jnp.exp(scores - log_totals[block_index])
        low_weights = weights.astype(bf16)
        weight_grad = jnp.einsum("qhd,khd->hqk", grad_block, value_rows, preferred_element_type=f32)
        value_acc = value_acc + jnp.einsum(
            "hqk,qhd->khd", low_weights, grad_block, preferred_element_type=f32
        )
        score_grad = (
            weights * (weight_grad - jnp.sum(weights * weight_grad, axis=-1, keepdims=True))
        ).astype(bf16)
        query_grad = (
            jnp.einsum("hqk,khd->qhd", score_grad, key_rows, preferred_element_type=f32) * scale
        ).astype(bf16)
        key_acc = (
            key_acc
            + jnp.einsum("hqk,qhd->khd", score_grad, query_block, preferred_element_type=f32)
            * scale
        )
        return ((key_acc, value_acc), query_grad)

    zeros_heads = jnp.zeros(head_shape, f32)
    (key_acc, value_acc), query_grads = lax.scan(
        back_block, (zeros_heads, zeros_heads), jnp.arange(num_blocks, dtype=jnp.int32)
    )
    queries_grad = query_grads.reshape(num_slots, width)
    keys_grad = key_acc.astype(bf16).reshape(num_slots, width)
    values_grad = value_acc.astype(bf16).reshape(num_slots, width)
    query_wgrad = jnp.einsum("sd,se->de", tokens, queries_grad, preferred_element_type=f32)
    query_bgrad = col_sum(queries_grad)
    key_wgrad = jnp.einsum("sd,se->de", tokens, keys_grad, preferred_element_type=f32)
    value_wgrad = jnp.einsum("sd,se->de", tokens, values_grad, preferred_element_type=f32)
    value_bgrad = col_sum(values_grad)
    tokens_grad = first_grad + jnp.einsum(
        "se,de->sd", queries_grad, query_full, preferred_element_type=f32
    )
    tokens_grad = tokens_grad + jnp.einsum(
        "se,de->sd", keys_grad, key_full, preferred_element_type=f32
    )
    tokens_grad = tokens_grad + jnp.einsum(
        "se,de->sd", values_grad, value_full, preferred_element_type=f32
    )
    attn_shares = (
        lax.psum_scatter(query_wgrad, ("dp", "fsdp"), scatter_dimension=0, tiled=True),
        lax.psum_scatter(key_wgrad, ("dp", "fsdp"), scatter_dimension=0, tiled=True),
        lax.psum_scatter(value_wgrad, ("dp", "fsdp"), scatter_dimension=0, tiled=True),
        lax.psum_scatter(mixer_wgrad, ("dp", "fsdp"), scatter_dimension=0, tiled=True),
        lax.psum_scatter(query_bgrad, ("dp", "fsdp"), scatter_dimension=0, tiled=True),
        lax.psum_scatter(value_bgrad, ("dp", "fsdp"), scatter_dimension=0, tiled=True),
        lax.psum_scatter(mixer_bgrad, ("dp", "fsdp"), scatter_dimension=0, tiled=True),
        lax.psum_scatter(again_grad, ("dp", "fsdp"), scatter_dimension=0, tiled=True),
        lax.psum_scatter(ashift_grad, ("dp", "fsdp"), scatter_dimension=0, tiled=True),
    )
    return (
        layer_out,
        tokens_grad,
        attn_shares[0],
        attn_shares[1],
        attn_shares[2],
        attn_shares[3],
        attn_shares[4],
        attn_shares[5],
        attn_shares[6],
        attn_shares[7],
        attn_shares[8],
        ffn_shares[0],
        ffn_shares[1],
        ffn_shares[2],
        ffn_shares[3],
        ffn_shares[4],
        ffn_shares[5],
    )


def solution(mesh):
    return jax.shard_map(
        local,
        mesh=mesh,
        in_specs=(
            P(("dp", "fsdp"), None),
            P(("dp", "fsdp"), None),
            P(("dp", "fsdp"), None),
            P(("dp", "fsdp"), None),
            P(("dp", "fsdp"), None),
            P(("dp", "fsdp"), None),
            P(("dp", "fsdp"), None),
            P(("dp", "fsdp")),
            P(("dp", "fsdp")),
            P(("dp", "fsdp")),
            P(("dp", "fsdp")),
            P(("dp", "fsdp")),
            P(("dp", "fsdp"), None),
            P(("dp", "fsdp")),
            P(("dp", "fsdp"), None),
            P(("dp", "fsdp")),
            P(("dp", "fsdp")),
            P(("dp", "fsdp")),
        ),
        out_specs=(
            P(("dp", "fsdp"), None),
            P(("dp", "fsdp"), None),
            P(("dp", "fsdp"), None),
            P(("dp", "fsdp"), None),
            P(("dp", "fsdp"), None),
            P(("dp", "fsdp"), None),
            P(("dp", "fsdp")),
            P(("dp", "fsdp")),
            P(("dp", "fsdp")),
            P(("dp", "fsdp")),
            P(("dp", "fsdp")),
            P(("dp", "fsdp"), None),
            P(("dp", "fsdp")),
            P(("dp", "fsdp"), None),
            P(("dp", "fsdp")),
            P(("dp", "fsdp")),
            P(("dp", "fsdp")),
        ),
        check_vma=False,
    )
```

profile of v0, /device:TPU:14, one launch (start us, length us, event | category | flops | bytes accessed | tf_op | source)
XLA Modules:
  0.0 1645.1 jit_solution(11013215268762667739)
XLA Ops:
  18.0 40.7 %all-reduce.18 = (bf16[1024]{0:T(1024)(128)(2,1)S(1)}, bf16[1024]{0:T(1024)(128)(2,1)S(1)}, bf16[1024]{0:T(1024)(128)(2,1)S(1)}, bf16[1024]{0:T(1024)(128)(2,1)S...) all-reduce(bf16[1024]{0:T(1024)(128)(2,1)S(1)} %dynamic-update-slic, ...), channel_id=1, replica_groups=mesh['dp'=8,'fsdp'=4] {'dp','fsdp'}, use_global_device_ids=true, to_apply=%add.2 | all-reduce | flops 8192 | bytes 32768
  66.0 28.6 %all-gather = bf16[32,1,128]{2,1,0:T(2,128)(2,1)S(1)} all-gather(bf16[1,1,128]{2,1,0:T(2,128)(2,1)S(1)} %bitcast.153), channel_id=1, replica_groups=mesh['dp'=8,'fsdp'=4] {'dp','fsdp'}, dimensions={0}, use_global_device_ids=true | all-gather | bytes 8448 | tf_op jit(solution)/shard_map/all_gather | solution.py:116
  105.4 19.9 %all-gather.8.cloned.1.call-done = bf16[1024,1024]{1,0:T(8,128)(2,1)} async-done(((bf16[32,1024]{1,0:T(8,128)(2,1)}), bf16[1024,1024]{1,0:T(8,128)(2,1)}) %all-gather.8.cloned.1.call-update) | async-done | bytes 2097168 | tf_op jit(solution)/shard_map/all_gather | solution.py:104
  131.3 52.1 %all-gather.12.cloned.1.call-done = bf16[1024,1024]{1,0:T(8,128)(2,1)} async-done(((bf16[32,1024]{1,0:T(8,128)(2,1)}), bf16[1024,1024]{1,0:T(8,128)(2,1)}) %all-gather.12.cloned.1.call-update) | async-done | bytes 2097168 | tf_op jit(solution)/shard_map/all_gather | solution.py:106
  190.9 98.8 %while.28 = (s32[]{:T(128)}, bf16[2,512,16,64]{1,3,2,0:T(8,128)(2,1)}, f32[2,16,512,1]{2,1,3,0:T(8,128)S(1)}, s32[2]{0:T(128)S(1)}, s32[1024]{0:T(1024)S(1)}, /*...) while((s32[]{:T(128)}, ...), condition=%wide.region_5.6_spmd.clone, body=%wide.region_2.5_spmd.clone.sunk | while | flops 2242373120 | bytes 109331160 | solution.py:149
  193.9 15.3 fusion.133
  209.2 14.9 exponential_reduce_fusion.2
  224.2 16.2 fusion.134
  243.0 15.6 fusion.133
  258.6 15.1 exponential_reduce_fusion.2
  273.7 15.9 fusion.134
  304.4 16.7 %all-gather.16.cloned.1.call-done = bf16[1024,4096]{1,0:T(8,128)(2,1)} async-done(((bf16[32,4096]{1,0:T(8,128)(2,1)}), bf16[1024,4096]{1,0:T(8,128)(2,1)}) %all-gather.16.cloned.1.call-update) | async-done | bytes 8388624 | tf_op jit(solution)/shard_map/all_gather | solution.py:115
  321.1 47.4 %fusion.39 = (bf16[1024,4096]{1,0:T(8,128)(2,1)}, f32[1024,4096]{1,0:T(8,128)}) fusion(f32[4096]{0:T(1024)S(1)} %bitcast.151, bf16[1024,4096]{1,0:T(8,128)(2,1)} %all-gather.16.cloned.1.call-done, bf16[1024,1024]{0,1:T(8,128)(2,1)S(1)} %fusion.65.clone.4), kind=kOutput, calls=%fused_computation.54 | convolution fusion | flops 8866758656 | bytes 35667968 | tf_op jit(solution)/shard_map/dot_general | solution.py:156
  368.5 31.5 %all-gather.18.cloned.1.call-done = bf16[4096,1024]{1,0:T(8,128)(2,1)} async-done(((bf16[128,1024]{1,0:T(8,128)(2,1)}), bf16[4096,1024]{1,0:T(8,128)(2,1)}) %all-gather.18.cloned.1.call-update) | async-done | bytes 8388624 | tf_op jit(solution)/shard_map/all_gather | solution.py:117
  400.0 14.9 fusion.68
  423.8 19.9 %convert_reduce_fusion = (f32[4096]{0:T(1024)}, bf16[1024,4096]{1,0:T(8,128)(2,1)}) fusion(f32[1024,4096]{1,0:T(8,128)} %get-tuple-element.367, f32[4096]{0:T(1024)S(1)} %bitcast.152, bf16[1024,1024]{0,1:T(8,128)(2,1)S(1)} %get-tuple-element.354, bf16[4096,1024]{1,0:T(8,128)(2,1)S(1)} %bitcast.156), kind=kOutput, calls=%fused_computation.61 | convolution fusion | flops 8644456448 | bytes 35684352 | tf_op jit(solution)/shard_map/sd,fd->sf/dot_general | solution.py:178
  443.8 16.9 %multiply_reduce_fusion.2 = (f32[1024]{0:T(1024)}, f32[1024]{0:T(1024)S(1)}, f32[1024]{0:T(1024)S(1)}, f32[1024]{0:T(1024)}, f32[1024,1024]{0,1:T(8,128)S(1)}) fusion(f32[1024,1024]{0,1:T(8,128)S(1)} %copy-done.5, f32[1024]{0:T(1024)S(1)} %add_rsqrt_fusion.1, f32[1024]{0:T(1024)S(1)} %broadcast_multiply_fusion.5, f32[1024]{0:T(1024)S(1)} %copy-done.30, ...), kind=kOutput, calls=%fused_computation.79 | convolution fusion | flops 8609853440 | bytes 31510528 | tf_op jit(solution)/shard_map/sf,df->sd/dot_general | solution.py:182
  468.0 223.7 %while.29 = (s32[]{:T(128)}, f32[1024,16,64]{0,2,1:T(8,128)}, f32[1024,16,64]{0,2,1:T(8,128)}, bf16[2,512,16,64]{1,3,2,0:T(8,128)(2,1)}, s32[2]{0:T(128)S(1)}, /...) while((s32[]{:T(128)}, f32[1024,16,64]{0,2,1:T(8,128)}, ...), condition=%wide.region_16.17_spmd.clone, body=%wide.region_14.16_spmd.clone.sunk | while | flops 5502920192 | bytes 357811072 | solution.py:231
  487.2 25.9 %multiply_reduce_fusion.9 = (f32[16,512]{1,0:T(8,128)S(1)}, f32[16,512,1024]{2,1,0:T(8,128)}) fusion(f32[16,512,1024]{2,1,0:T(8,128)} %fusion.144, f32[16,512]{1,0:T(8,128)S(1)} %dynamic-slice_bitcast_fusion.2, pred[512,1024]{1,0:T(8,128)(4,1)S(1)} %fusion.145, bf16[1024,16,64]{0,2,1:T(8,128)(2,1)} %get-tuple-element.616, ...), kind=kOutput, calls=%fused_computation.23.clone.1 | convolution fusion | flops 1115676672 | bytes 70844416 | tf_op jit(solution)/shard_map/while/body/eval_jaxpr/qhd,khd->hqk/dot_general | solution.py:213
  513.1 27.8 %multiply_convert_fusion.3 = bf16[16,512,1024]{2,1,0:T(8,128)(2,1)} fusion(f32[16,512,1024]{2,1,0:T(8,128)} %get-tuple-element.525, f32[16,512,1024]{2,1,0:T(8,128)} %fusion.144, f32[16,512]{1,0:T(8,128)S(1)} %get-tuple-element.526, f32[16,512]{1,0:T(8,128)S(1)} %dynamic-slice_bitcast_fusion.2, pred[512,1024]{1,0:T(8,128)(4,1)S(1)} %fusion.145), kind=kLoop, calls=%fused_computation.22.clone.1 | loop fusion | flops 50331648 | bytes 84475904 | tf_op jit(solution)/shard_map/while/body/eval_jaxpr/convert_element_type | solution.py:219
  561.0 17.6 %bitcast_add_fusion.5 = f32[1024,16,64]{0,2,1:T(8,128)} fusion(f32[1024,16,64]{0,2,1:T(8,128)} %get-tuple-element.589, f32[16,512,1024]{2,1,0:T(8,128)} %fusion.144, f32[16,512]{1,0:T(8,128)S(1)} %dynamic-slice_bitcast_fusion.2, pred[512,1024]{1,0:T(8,128)(4,1)S(1)} %fusion.145, pred[]{:T(512)S(6)} %compare.3, ...), kind=kOutput, calls=%fused_computation.28.clone.1 | convolution fusion | flops 1109393408 | bytes 43548676 | tf_op jit(solution)/shard_map/while/body/eval_jaxpr/hqk,qhd->khd/dot_general | solution.py:214
  597.6 25.9 %multiply_reduce_fusion.9 = (f32[16,512]{1,0:T(8,128)S(1)}, f32[16,512,1024]{2,1,0:T(8,128)}) fusion(f32[16,512,1024]{2,1,0:T(8,128)} %fusion.144, f32[16,512]{1,0:T(8,128)S(1)} %dynamic-slice_bitcast_fusion.2, pred[512,1024]{1,0:T(8,128)(4,1)S(1)} %fusion.145, bf16[1024,16,64]{0,2,1:T(8,128)(2,1)} %get-tuple-element.616, ...), kind=kOutput, calls=%fused_computation.23.clone.1 | convolution fusion | flops 1115676672 | bytes 70844416 | tf_op jit(solution)/shard_map/while/body/eval_jaxpr/qhd,khd->hqk/dot_general | solution.py:213
  623.5 27.8 %multiply_convert_fusion.3 = bf16[16,512,1024]{2,1,0:T(8,128)(2,1)} fusion(f32[16,512,1024]{2,1,0:T(8,128)} %get-tuple-element.525, f32[16,512,1024]{2,1,0:T(8,128)} %fusion.144, f32[16,512]{1,0:T(8,128)S(1)} %get-tuple-element.526, f32[16,512]{1,0:T(8,128)S(1)} %dynamic-slice_bitcast_fusion.2, pred[512,1024]{1,0:T(8,128)(4,1)S(1)} %fusion.145), kind=kLoop, calls=%fused_computation.22.clone.1 | loop fusion | flops 50331648 | bytes 84475904 | tf_op jit(solution)/shard_map/while/body/eval_jaxpr/convert_element_type | solution.py:219
  672.5 18.8 %bitcast_add_fusion.5 = f32[1024,16,64]{0,2,1:T(8,128)} fusion(f32[1024,16,64]{0,2,1:T(8,128)} %get-tuple-element.589, f32[16,512,1024]{2,1,0:T(8,128)} %fusion.144, f32[16,512]{1,0:T(8,128)S(1)} %dynamic-slice_bitcast_fusion.2, pred[512,1024]{1,0:T(8,128)(4,1)S(1)} %fusion.145, pred[]{:T(512)S(6)} %compare.3, ...), kind=kOutput, calls=%fused_computation.28.clone.1 | convolution fusion | flops 1109393408 | bytes 43548676 | tf_op jit(solution)/shard_map/while/body/eval_jaxpr/hqk,qhd->khd/dot_general | solution.py:214
  743.3 16.9 %fusion.62 = f32[1024,4096]{1,0:T(8,128)} fusion(bf16[1024,4096]{1,0:T(8,128)(2,1)} %get-tuple-element.372, f32[1024,1024]{0,1:T(8,128)} %copy-done.4, f32[1024]{0:T(1024)S(1)} %copy-done.40, f32[1024]{0:T(1024)S(1)} %copy-done.31, f32[1024]{0:T(1024)S(1)} %copy-done.33, f32[1024]{0:T(1024)S(1)} %copy-done.27), kind=kOutput, calls=%fused_computation.126 | convolution fusion | flops 8595177472 | bytes 29376512 | tf_op jit(solution)/shard_map/sd,sf->df/dot_general | solution.py:180
  761.7 14.6 fusion.69
  778.4 41.3 %all-reduce.17 = (f32[1024]{0:T(1024)S(1)}, f32[1024]{0:T(1024)S(1)}, f32[1024]{0:T(1024)S(1)}, f32[1024]{0:T(1024)S(1)}, f32[1024]{0:T(1024)S(1)}, /*index=5*/f...) all-reduce(f32[1024]{0:T(1024)S(1)} %reduce_sum.197, ...), channel_id=6, replica_groups=mesh['dp'=8,'fsdp'=4] {'dp','fsdp'}, use_global_device_ids=true, to_apply=%region_22.23.clone | all-reduce | flops 12288 | bytes 98304
  845.7 109.2 %reduce-scatter.23.cloned.1.call-done = f32[32,1024]{1,0:T(8,128)} async-done(((f32[1024,1024]{1,0:T(8,128)}), f32[32,1024]{1,0:T(8,128)}) %reduce-scatter.23.cloned.1.call-update) | async-done | bytes 131088
  954.9 139.8 %reduce-scatter.21.cloned.1.call-done = f32[32,1024]{1,0:T(8,128)} async-done(((f32[1024,1024]{1,0:T(8,128)}), f32[32,1024]{1,0:T(8,128)}) %reduce-scatter.21.cloned.1.call-update) | async-done | bytes 131088
  1094.7 139.8 %reduce-scatter.13.cloned.1.call-done = f32[32,1024]{1,0:T(8,128)} async-done(((f32[1024,1024]{1,0:T(8,128)}), f32[32,1024]{1,0:T(8,128)}) %reduce-scatter.13.cloned.1.call-update) | async-done | bytes 131088 | tf_op jit(solution)/shard_map/reduce_scatter | solution.py:255
  1234.5 216.2 %reduce-scatter.15.cloned.1.call-done = f32[32,4096]{1,0:T(8,128)} async-done(((f32[1024,4096]{1,0:T(8,128)}), f32[32,4096]{1,0:T(8,128)}) %reduce-scatter.15.cloned.1.call-update) | async-done | bytes 524304 | tf_op jit(solution)/shard_map/reduce_scatter | solution.py:186
  1450.7 187.3 %reduce-scatter.17.cloned.1.call-done = f32[128,1024]{1,0:T(8,128)} async-done(((f32[4096,1024]{1,0:T(8,128)}), f32[128,1024]{1,0:T(8,128)}) %reduce-scatter.17.cloned.1.call-update) | async-done | bytes 524304 | tf_op jit(solution)/shard_map/reduce_scatter | solution.py:188
  (252 shorter events, 231.9 us)
Async XLA Ops:
  7.2 58.8 %copy-start.47 = (bf16[128]{0:T(256)(128)(2,1)S(1)}, bf16[128]{0:T(256)(128)(2,1)}, u32[]{:S(2)}) copy-start(bf16[128]{0:T(256)(128)(2,1)} %param.35) | copy-start | bytes 772
  7.2 90.4 %copy-start.18 = (bf16[1024,1024]{1,0:T(8,128)(2,1)S(1)}, bf16[1024,1024]{1,0:T(8,128)(2,1)}, u32[]{:S(2)}) copy-start(bf16[1024,1024]{1,0:T(8,128)(2,1)} %param.24) | copy-start | bytes 6291460
  7.2 93.5 %all-gather.10.cloned.1.call-start = ((), (), s32[]{:S(2)}) async-start(), calls=%async_computation.7 | async-start | bytes 2162688 | tf_op jit(solution)/shard_map/all_gather | solution.py:105
  7.9 117.3 %all-gather.8.cloned.1.call-start = ((), (), s32[]{:S(2)}) async-start(), calls=%async_computation.6 | async-start | bytes 2162688 | tf_op jit(solution)/shard_map/all_gather | solution.py:104
  8.7 174.7 %all-gather.12.cloned.1.call-start = ((), (), s32[]{:S(2)}) async-start(), calls=%async_computation.8 | async-start | bytes 2162688 | tf_op jit(solution)/shard_map/all_gather | solution.py:106
  9.4 286.7 %all-gather.14.cloned.1.call-start = ((), (), s32[]{:S(2)}) async-start(), calls=%async_computation.9 | async-start | bytes 2162688 | tf_op jit(solution)/shard_map/all_gather | solution.py:107
  10.0 311.1 %all-gather.16.cloned.1.call-start = ((), (), s32[]{:S(2)}) async-start(), calls=%async_computation.10 | async-start | bytes 8650752 | tf_op jit(solution)/shard_map/all_gather | solution.py:115
  10.6 389.4 %all-gather.18.cloned.1.call-start = ((), (), s32[]{:S(2)}) async-start(), calls=%async_computation.11 | async-start | bytes 8650752 | tf_op jit(solution)/shard_map/all_gather | solution.py:117
  11.2 834.5 %reduce-scatter.19.cloned.1.call-start = ((), (), s32[]{:S(2)}) async-start(), calls=%async_computation.15 | async-start | bytes 4325376
  289.7 6.5 copy-start.1
  289.7 6.5 copy-start.22
  289.7 6.5 copy-start.24
  289.7 6.5 copy-start.46
  301.8 158.9 %copy-start.26 = (f32[1024]{0:T(1024)}, f32[1024]{0:T(1024)S(1)}, u32[]{:S(2)}) copy-start(f32[1024]{0:T(1024)S(1)} %broadcast_multiply_fusion.5) | copy-start | bytes 12292
  302.2 18.9 %copy-start.42 = (f32[32,1,128]{2,1,0:T(1,128)S(1)}, f32[32,1,128]{2,1,0:T(1,128)}, u32[]{:S(2)}) copy-start(f32[32,1,128]{2,1,0:T(1,128)} %convert_element_type.158) | copy-start | bytes 49156
  303.7 156.9 %copy-start.32 = (f32[1024]{0:T(1024)}, f32[1024]{0:T(1024)S(1)}, u32[]{:S(2)}) copy-start(f32[1024]{0:T(1024)S(1)} %add_rsqrt_fusion.1) | copy-start | bytes 12292
  321.1 78.8 %copy-start.45 = (f32[1024]{0:T(1024)S(1)}, f32[1024]{0:T(1024)}, u32[]{:S(2)}) copy-start(f32[1024]{0:T(1024)} %convert_element_type.141) | copy-start | bytes 12292
  416.5 7.3 slice-start
  423.8 20.0 %copy-start.14 = (bf16[1024,1024]{0,1:T(8,128)(2,1)}, bf16[1024,1024]{0,1:T(8,128)(2,1)S(1)}, u32[]{:S(2)}) copy-start(bf16[1024,1024]{0,1:T(8,128)(2,1)S(1)} %get-tuple-element.354) | copy-start | bytes 6291460
  423.8 20.0 %copy-start.5 = (f32[1024,1024]{0,1:T(8,128)S(1)}, f32[1024,1024]{0,1:T(8,128)}, u32[]{:S(2)}) copy-start(f32[1024,1024]{0,1:T(8,128)} %copy-done.4) | copy-start | bytes 12582916
  462.7 5.3 copy-start.23
  540.9 12.3 copy-start
  561.0 17.6 %copy-start.3 = (bf16[1024,16,64]{0,2,1:T(8,128)(2,1)S(1)}, bf16[1024,16,64]{0,2,1:T(8,128)(2,1)}, u32[]{:S(2)}) copy-start(bf16[1024,16,64]{0,2,1:T(8,128)(2,1)} %get-tuple-element.654) | copy-start | bytes 6291460 | tf_op jit(solution)/shard_map/while
  651.3 13.5 copy-start
  672.5 18.8 %copy-start.3 = (bf16[1024,16,64]{0,2,1:T(8,128)(2,1)S(1)}, bf16[1024,16,64]{0,2,1:T(8,128)(2,1)}, u32[]{:S(2)}) copy-start(bf16[1024,16,64]{0,2,1:T(8,128)(2,1)} %get-tuple-element.654) | copy-start | bytes 6291460 | tf_op jit(solution)/shard_map/while
  691.7 5.8 copy-start.19
  707.3 247.6 %reduce-scatter.23.cloned.1.call-start = ((), (), s32[]{:S(2)}) async-start(), calls=%async_computation.17 | async-start | bytes 4325376
  720.9 373.8 %reduce-scatter.21.cloned.1.call-start = ((), (), s32[]{:S(2)}) async-start(), calls=%async_computation.16 | async-start | bytes 4325376
  734.5 500.1 %reduce-scatter.13.cloned.1.call-start = ((), (), s32[]{:S(2)}) async-start(), calls=%async_computation.12 | async-start | bytes 4325376 | tf_op jit(solution)/shard_map/reduce_scatter | solution.py:255
  742.6 708.1 %reduce-scatter.15.cloned.1.call-start = ((), (), s32[]{:S(2)}) async-start(), calls=%async_computation.13 | async-start | bytes 17301504 | tf_op jit(solution)/shard_map/reduce_scatter | solution.py:186
  760.2 877.8 %reduce-scatter.17.cloned.1.call-start = ((), (), s32[]{:S(2)}) async-start(), calls=%async_computation.14 | async-start | bytes 17301504 | tf_op jit(solution)/shard_map/reduce_scatter | solution.py:188
  837.0 5.5 copy-start.10
  (34 other events, 79.5 us)
Sparse Core Ops, SparseCore 0:
  10.9 56.0 all-gather.9
  69.8 55.4 all-gather.7
  128.1 55.2 all-gather.11
  186.1 55.2 all-gather.13
  244.1 76.9 all-gather.15
  323.9 76.0 all-gather.17
  707.4 108.1 reduce-scatter.18
  818.5 136.3 reduce-scatter.22
  957.7 136.8 reduce-scatter.20
  1097.4 137.0 reduce-scatter.12
  1237.4 213.2 reduce-scatter.14
  1453.4 184.5 reduce-scatter.16
where the time goes:
time: 1660 us; the launch traced here: 1650 us
  waiting for transfers between devices  916 us (55%)
  matrix products  407 us (25%)
  other arithmetic  114 us (7%)
  blocking collectives  111 us (7%)
  local copies, waits for them, and re-layouts  74.7 us (4%)
    unnamed x15, waiting for transfers between devices  253 us
    reduce_scatter x1, waiting for transfers between devices, local(): lax.psum_scatter(inner_wgrad, ('dp', 'fsdp'), scatter_dimension=0, tiled=...  216 us
    reduce_scatter x1, waiting for transfers between devices, local(): lax.psum_scatter(outer_wgrad, ('dp', 'fsdp'), scatter_dimension=0, tiled=...  187 us
    reduce_scatter x1, waiting for transfers between devices, local(): lax.psum_scatter(mixer_wgrad, ('dp', 'fsdp'), scatter_dimension=0, tiled=...  140 us
    unnamed x2, blocking collectives  82 us
    dot_general x4, matrix products, masked_scores(): jnp.einsum('qhd,khd->hqk', query_block, key_rows, preferred_element_type=...  59.7 us
    unnamed x134, local copies, waits for them, and re-layouts  57.9 us
    convert_element_type x2, other arithmetic, back_block(): score_grad = (weights * (weight_grad - jnp.sum(weights * weight_grad, axi...  55.6 us
  transfers between devices with their start and end apart: 12, of which 9 were waited for; matrix products, arithmetic and copies ran while one was open for 17% of the time, Pallas kernels for 0%

commit v1 on v0

v1 whole, which is shorter than its diff:
```python
import jax
import jax.numpy as jnp
from jax import lax
from jax.experimental import pallas as pl
from jax.experimental.pallas import tpu as pltpu
from jax.sharding import PartitionSpec as P

HEAD_DIM = 64


EPS = 1e-06
NEG = -1e30


def slot_layout(lengths, num_rows):
    bounds = jnp.cumsum(lengths, axis=-1)
    position = jnp.arange(num_rows, dtype=jnp.int32)
    segment = jnp.sum((position[:, None] >= bounds[..., None, :]).astype(jnp.int32), axis=-1)
    usable = position < bounds[..., -1:]
    return (segment, usable)


def norm_forward(values_in, gain_vec, shift_vec):
    average = jnp.mean(values_in, axis=-1, keepdims=True)
    centred = values_in - average
    inv_std = lax.rsqrt(jnp.mean(centred * centred, axis=-1, keepdims=True) + EPS)
    normed = centred * inv_std
    return (normed * gain_vec.astype(jnp.float32) + shift_vec.astype(jnp.float32), normed, inv_std)


def norm_back(incoming, normed, inv_std, gain_vec):
    scaled = incoming * gain_vec.astype(jnp.float32)
    first_mean = jnp.mean(scaled, axis=-1, keepdims=True)
    second_mean = jnp.mean(scaled * normed, axis=-1, keepdims=True)
    values_grad = inv_std * (scaled - first_mean - normed * second_mean)
    return (values_grad, jnp.sum(incoming * normed, axis=0), jnp.sum(incoming, axis=0))


def gelu_slope(inner):
    return 0.5 * (1.0 + lax.erf(inner * 2.0 ** (-0.5))) + inner * jnp.exp(-0.5 * inner * inner) * (
        2.0 * jnp.pi
    ) ** (-0.5)


def dot_last(left, right):
    return lax.dot_general(left, right, (((1,), (1,)), ((), ())), preferred_element_type=jnp.float32)


def dot_first(left, right):
    return lax.dot_general(left, right, (((0,), (0,)), ((), ())), preferred_element_type=jnp.float32)


def attend_kernel(low_ref, high_ref, q_ref, k_ref, v_ref, idcol_ref, idrow_ref, o_ref, lse_ref):
    block = q_ref.shape[0]
    at = pl.program_id(1)
    f32 = jnp.float32
    scale = HEAD_DIM ** (-0.5)
    lane_key = lax.broadcasted_iota(jnp.int32, (block, 2 * HEAD_DIM), 1)
    first_head = lane_key < HEAD_DIM
    queries = (q_ref[...].astype(f32) * scale).astype(jnp.bfloat16)
    row_id = idcol_ref[...][:, :1]

    def step(kb, carry):
        place = pl.ds(pl.multiple_of(kb * block, block), block)
        keys = k_ref[place, :]
        vals = v_ref[place, :]
        same = row_id == idrow_ref[:1, place]
        out = []
        for head in range(2):
            top, total, acc = carry[head]
            mine = first_head if head == 0 else jnp.logical_not(first_head)
            scores = dot_last(queries, jnp.where(mine, keys, jnp.zeros_like(keys)))
            scores = jnp.where(same, scores, NEG)
            new_top = jnp.maximum(top, jnp.max(scores, axis=1, keepdims=True))
            fade = jnp.exp(top - new_top)
            weights = jnp.exp(scores - new_top)
            total = fade * total + jnp.sum(weights, axis=1, keepdims=True)
            acc = fade * acc + jnp.dot(
                weights.astype(jnp.bfloat16),
                jnp.where(mine, vals, jnp.zeros_like(vals)),
                preferred_element_type=f32,
            )
            out.append((new_top, total, acc))
        return tuple(out)

    start = (
        jnp.full((block, 1), NEG, f32),
        jnp.zeros((block, 1), f32),
        jnp.zeros((block, 2 * HEAD_DIM), f32),
    )
    one, two = lax.fori_loop(low_ref[at], high_ref[at], step, (start, start))
    o_ref[...] = (one[2] / one[1] + two[2] / two[1]).astype(o_ref.dtype)
    lse = jnp.where(first_head, one[0] + jnp.log(one[1]), two[0] + jnp.log(two[1])).T
    lse_ref[0, 0:1, :] = lse[0:1]
    lse_ref[0, 1:2, :] = lse[HEAD_DIM : HEAD_DIM + 1]


def attend_back_kernel(
    low_ref, high_ref, q_ref, k_ref, v_ref, g_ref, o_ref, lse_ref, idcol_ref, idrow_ref,
    dq_ref, dk_ref, dv_ref, dq_acc, delta_ref,
):
    block = k_ref.shape[0]
    at = pl.program_id(1)
    f32 = jnp.float32
    bf16 = jnp.bfloat16
    scale = HEAD_DIM ** (-0.5)
    lane_key = lax.broadcasted_iota(jnp.int32, (block, 2 * HEAD_DIM), 1)
    first_head = lane_key < HEAD_DIM

    @pl.when(at == 0)
    def _():
        dq_acc[...] = jnp.zeros_like(dq_acc)
        both = (g_ref[...].astype(f32) * o_ref[...].astype(f32)).T
        delta_ref[0:1, :] = jnp.sum(both[:HEAD_DIM], axis=0, keepdims=True)
        delta_ref[1:2, :] = jnp.sum(both[HEAD_DIM:], axis=0, keepdims=True)

    keys = k_ref[...]
    vals = v_ref[...]
    none = jnp.zeros_like(keys)
    key_of = (jnp.where(first_head, keys, none), jnp.where(first_head, none, keys))
    val_of = (jnp.where(first_head, vals, none), jnp.where(first_head, none, vals))
    key_id = idcol_ref[...][:, :1]

    def step(qb, carry):
        place = pl.ds(pl.multiple_of(qb * block, block), block)
        queries = (q_ref[place, :].astype(f32) * scale).astype(bf16)
        grads = g_ref[place, :]
        same = key_id == idrow_ref[:1, place]
        out = []
        dq = dq_acc[place, :]
        for head in range(2):
            dk, dv = carry[head]
            scores = dot_last(key_of[head], queries)
            weights = jnp.exp(jnp.where(same, scores - lse_ref[0, head : head + 1, place], NEG))
            weight_grad = dot_last(val_of[head], grads)
            dv = dv + jnp.dot(weights.astype(bf16), grads, preferred_element_type=f32)
            score_grad = (weights * (weight_grad - delta_ref[head : head + 1, place])).astype(bf16)
            dk = dk + jnp.dot(score_grad, queries, preferred_element_type=f32)
            dq = dq + dot_first(score_grad, key_of[head])
            out.append((dk, dv))
        dq_acc[place, :] = dq
        return tuple(out)

    zero = jnp.zeros((block, 2 * HEAD_DIM), f32)
    one, two = lax.fori_loop(low_ref[at], high_ref[at], step, ((zero, zero), (zero, zero)))
    dk_ref[...] = jnp.where(first_head, one[0], two[0]).astype(bf16)
    dv_ref[...] = jnp.where(first_head, one[1], two[1]).astype(bf16)

    @pl.when(at == pl.num_programs(1) - 1)
    def _():
        dq_ref[...] = (dq_acc[...] * scale).astype(bf16)


def attention_plan(segment, usable, block):
    num_slots = segment.shape[0]
    position = jnp.arange(num_slots, dtype=jnp.int32)
    ident = jnp.where(usable, segment, num_slots + position)
    same = ident[:, None] == ident[None, :]
    num_blocks = num_slots // block
    met = jnp.any(same.reshape(num_blocks, block, num_blocks, block), axis=(1, 3))
    order = jnp.arange(num_blocks, dtype=jnp.int32)[None, :]
    first = jnp.min(jnp.where(met, order, num_blocks), axis=1)
    last = jnp.max(jnp.where(met, order + 1, 0), axis=1)
    column = jnp.broadcast_to(ident[:, None], (num_slots, 128))
    row = jnp.broadcast_to(ident[None, :], (8, num_slots))
    return first, last, column, row


def attend(plan, queries, keys, vals, block):
    num_slots, width = queries.shape
    pairs = width // (2 * HEAD_DIM)
    first, last, column, row = plan
    lanes = 2 * HEAD_DIM
    part = pl.BlockSpec((block, lanes), lambda p, b, *_: (b, p))
    full = pl.BlockSpec((num_slots, lanes), lambda p, b, *_: (0, p))
    return pl.pallas_call(
        attend_kernel,
        grid_spec=pltpu.PrefetchScalarGridSpec(
            num_scalar_prefetch=2,
            grid=(pairs, num_slots // block),
            in_specs=[
                part, full, full,
                pl.BlockSpec((block, 128), lambda p, b, *_: (b, 0)),
                pl.BlockSpec((8, num_slots), lambda p, b, *_: (0, 0)),
            ],
            out_specs=[part, pl.BlockSpec((1, 2, block), lambda p, b, *_: (p, 0, b))],
        ),
        out_shape=[
            jax.ShapeDtypeStruct((num_slots, width), jnp.bfloat16),
            jax.ShapeDtypeStruct((pairs, 2, num_slots), jnp.float32),
        ],
        compiler_params=pltpu.CompilerParams(vmem_limit_bytes=32 * 2**20),
        cost_estimate=pl.CostEstimate(
            flops=4 * num_slots * num_slots * width,
            bytes_accessed=8 * num_slots * width,
            transcendentals=num_slots * num_slots * width // HEAD_DIM,
        ),
        name="attend",
    )(first, last, queries, keys, vals, column, row)


def attend_back(plan, queries, keys, vals, grads, attended, lse, block):
    num_slots, width = queries.shape
    pairs = width // (2 * HEAD_DIM)
    first, last, column, row = plan
    lanes = 2 * HEAD_DIM
    part = pl.BlockSpec((block, lanes), lambda p, b, *_: (b, p))
    full = pl.BlockSpec((num_slots, lanes), lambda p, b, *_: (0, p))
    return pl.pallas_call(
        attend_back_kernel,
        grid_spec=pltpu.PrefetchScalarGridSpec(
            num_scalar_prefetch=2,
            grid=(pairs, num_slots // block),
            in_specs=[
                full, part, part, full, full,
                pl.BlockSpec((1, 2, num_slots), lambda p, b, *_: (p, 0, 0)),
                pl.BlockSpec((block, 128), lambda p, b, *_: (b, 0)),
                pl.BlockSpec((8, num_slots), lambda p, b, *_: (0, 0)),
            ],
            out_specs=[full, part, part],
            scratch_shapes=[
                pltpu.VMEM((num_slots, lanes), jnp.float32),
                pltpu.VMEM((8, num_slots), jnp.float32),
            ],
        ),
        out_shape=[jax.ShapeDtypeStruct((num_slots, width), jnp.bfloat16)] * 3,
        compiler_params=pltpu.CompilerParams(vmem_limit_bytes=32 * 2**20),
        cost_estimate=pl.CostEstimate(
            flops=10 * num_slots * num_slots * width,
            bytes_accessed=16 * num_slots * width,
            transcendentals=num_slots * num_slots * width // HEAD_DIM,
        ),
        name="attend_back",
    )(first, last, queries, keys, vals, grads, attended, lse, column, row)


def col_sum(array_in):
    return jnp.sum(array_in.astype(jnp.float32), axis=0)


def vec_rows(vectors, width):
    flat = jnp.concatenate([v.reshape(v.shape[0], -1) for v in vectors], axis=1)
    rows = -(-flat.shape[1] // (16 * width)) * 16
    flat = jnp.pad(flat, ((0, 0), (0, rows * width - flat.shape[1])))
    return flat.reshape(flat.shape[0], rows, width)


def pack(devices, matrices, vectors):
    width = matrices[0].shape[1]
    parts = [m.reshape(devices, -1, width) for m in matrices]
    parts.append(vec_rows([v.reshape(devices, -1) for v in vectors], width))
    return jnp.concatenate(parts, axis=1)


def unpack(packed, matrix_rows, vector_sizes):
    devices, _, width = packed.shape
    matrices, at = [], 0
    for rows in matrix_rows:
        matrices.append(packed[:, at : at + rows].reshape(devices * rows, width))
        at += rows
    flat = packed[:, at:].reshape(devices, -1)
    vectors, at = [], 0
    for size in vector_sizes:
        vectors.append(flat[:, at : at + size].reshape(-1))
        at += size
    return matrices, vectors


def gather(packed):
    return lax.all_gather(packed[0], ("dp", "fsdp"), axis=0, tiled=False)


def scatter_sum(packed):
    return lax.psum_scatter(packed, ("dp", "fsdp"), scatter_dimension=0, tiled=True)[0]


def column_parts(matrix, width):
    return [matrix[:, at : at + width] for at in range(0, matrix.shape[1], width)]


def local(
    tokens,
    lengths,
    cotangent,
    query_weight,
    key_weight,
    value_weight,
    mixer_weight,
    query_bias,
    value_bias,
    mixer_bias,
    attn_gain,
    attn_shift,
    inner_weight,
    inner_bias,
    outer_weight,
    outer_bias,
    final_gain,
    final_shift,
):
    num_slots = tokens.shape[0]
    width = tokens.shape[1]
    devices = width // query_weight.shape[0]
    block = min(256, num_slots)
    segment, usable = slot_layout(lengths, num_slots)
    segment = segment[0]
    usable = usable[0]
    f32 = jnp.float32
    bf16 = jnp.bfloat16
    rows = query_weight.shape[0]
    ff_rows = outer_weight.shape[0]
    splits = inner_weight.shape[1] // width
    attn_packed = pack(1, [query_weight, key_weight, value_weight], [query_bias, value_bias])
    rest_packed = pack(
        1,
        [mixer_weight, *column_parts(inner_weight, width), outer_weight],
        [mixer_bias, attn_gain, attn_shift, inner_bias, outer_bias, final_gain, final_shift],
    )
    attn_all, rest_packed = lax.optimization_barrier((gather(attn_packed), rest_packed))
    (query_full, key_full, value_full), (qbias_full, vbias_full) = unpack(
        attn_all, [rows] * 3, [rows] * 2
    )
    rest_mats, rest_vecs = unpack(
        gather(rest_packed),
        [rows] * (1 + splits) + [ff_rows],
        [rows] * 3 + [ff_rows] + [rows] * 3,
    )
    mixer_full, outer_full = rest_mats[0], rest_mats[-1]
    inner_full = jnp.concatenate(rest_mats[1:-1], axis=1)
    mbias_full, again_full, ashift_full, ibias_full, obias_full, fgain_full, fshift_full = rest_vecs

    queries = (
        jnp.dot(tokens, query_full, preferred_element_type=f32) + qbias_full.astype(f32)
    ).astype(bf16)
    key_rows = jnp.dot(tokens, key_full, preferred_element_type=f32).astype(bf16)
    value_rows = (
        jnp.dot(tokens, value_full, preferred_element_type=f32) + vbias_full.astype(f32)
    ).astype(bf16)
    plan = attention_plan(segment, usable, block)
    attended, lse = attend(plan, queries, key_rows, value_rows, block)
    mixed = jnp.dot(attended, mixer_full, preferred_element_type=f32) + mbias_full.astype(f32)
    hidden, first_normed, first_inv = norm_forward(
        tokens.astype(f32) + mixed, again_full, ashift_full
    )
    hidden_low = hidden.astype(bf16)
    inner = jnp.dot(hidden_low, inner_full, preferred_element_type=f32) + ibias_full.astype(f32)
    activated = (inner * (0.5 * (1.0 + lax.erf(inner * 2.0 ** (-0.5))))).astype(bf16)
    outer = jnp.dot(activated, outer_full, preferred_element_type=f32) + obias_full.astype(f32)
    final, second_normed, second_inv = norm_forward(hidden + outer, fgain_full, fshift_full)
    layer_out = final.astype(bf16)
    out_grad = cotangent.astype(f32) * usable[:, None].astype(f32)
    second_grad, fgain_grad, fshift_grad = norm_back(
        out_grad, second_normed, second_inv, fgain_full
    )
    outer_low = second_grad.astype(bf16)
    outer_wgrad = jnp.einsum("sf,sd->fd", activated, outer_low, preferred_element_type=f32)
    outer_bgrad = col_sum(outer_low)
    act_grad = jnp.einsum("sd,fd->sf", outer_low, outer_full, preferred_element_type=f32)
    inner_low = (act_grad * gelu_slope(inner)).astype(bf16)
    inner_wgrads = [
        jnp.einsum("sd,sf->df", hidden_low, part, preferred_element_type=f32).astype(bf16)
        for part in column_parts(inner_low, width)
    ]
    inner_bgrad = col_sum(inner_low)
    hidden_grad = second_grad + jnp.einsum(
        "sf,df->sd", inner_low, inner_full, preferred_element_type=f32
    )
    first_grad, again_grad, ashift_grad = norm_back(
        hidden_grad, first_normed, first_inv, again_full
    )
    mixed_low = first_grad.astype(bf16)
    mixer_wgrad = jnp.einsum("sa,sd->ad", attended, mixed_low, preferred_element_type=f32)
    mixer_bgrad = col_sum(mixed_low)
    attended_grad = jnp.einsum(
        "sd,ad->sa", mixed_low, mixer_full, preferred_element_type=f32
    ).astype(bf16)
    rest_grads = pack(
        devices,
        [mixer_wgrad.astype(bf16), *inner_wgrads, outer_wgrad.astype(bf16)],
        [
            g.astype(bf16)
            for g in (
                mixer_bgrad, again_grad, ashift_grad, inner_bgrad, outer_bgrad, fgain_grad, fshift_grad,
            )
        ],
    )
    rest_grads, attended_grad = lax.optimization_barrier((rest_grads, attended_grad))
    rest_sums = scatter_sum(rest_grads)
    queries_grad, keys_grad, values_grad = attend_back(
        plan, queries, key_rows, value_rows, attended_grad, attended, lse, block
    )
    wgrads = [
        jnp.einsum("sd,se->de", tokens, g, preferred_element_type=f32).astype(bf16)
        for g in (queries_grad, keys_grad, values_grad)
    ]
    attn_grads = pack(
        devices, wgrads, [col_sum(queries_grad).astype(bf16), col_sum(values_grad).astype(bf16)]
    )
    attn_grads, queries_grad, keys_grad, values_grad = lax.optimization_barrier(
        (attn_grads, queries_grad, keys_grad, values_grad)
    )
    attn_sums = scatter_sum(attn_grads)
    tokens_grad = first_grad + jnp.einsum(
        "se,de->sd", queries_grad, query_full, preferred_element_type=f32
    )
    tokens_grad = tokens_grad + jnp.einsum(
        "se,de->sd", keys_grad, key_full, preferred_element_type=f32
    )
    tokens_grad = tokens_grad + jnp.einsum(
        "se,de->sd", values_grad, value_full, preferred_element_type=f32
    )
    rest_mats, rest_vecs = unpack(
        rest_sums.astype(f32)[None],
        [rows] * (1 + splits) + [ff_rows],
        [rows] * 3 + [ff_rows] + [rows] * 3,
    )
    attn_mats, attn_vecs = unpack(attn_sums.astype(f32)[None], [rows] * 3, [rows] * 2)
    return (
        layer_out,
        tokens_grad,
        attn_mats[0],
        attn_mats[1],
        attn_mats[2],
        rest_mats[0],
        attn_vecs[0],
        attn_vecs[1],
        rest_vecs[0],
        rest_vecs[1],
        rest_vecs[2],
        jnp.concatenate(rest_mats[1:-1], axis=1),
        rest_vecs[3],
        rest_mats[-1],
        rest_vecs[4],
        rest_vecs[5],
        rest_vecs[6],
    )


def solution(mesh):
    return jax.shard_map(
        local,
        mesh=mesh,
        in_specs=(
            P(("dp", "fsdp"), None),
            P(("dp", "fsdp"), None),
            P(("dp", "fsdp"), None),
            P(("dp", "fsdp"), None),
            P(("dp", "fsdp"), None),
            P(("dp", "fsdp"), None),
            P(("dp", "fsdp"), None),
            P(("dp", "fsdp")),
            P(("dp", "fsdp")),
            P(("dp", "fsdp")),
            P(("dp", "fsdp")),
            P(("dp", "fsdp")),
            P(("dp", "fsdp"), None),
            P(("dp", "fsdp")),
            P(("dp", "fsdp"), None),
            P(("dp", "fsdp")),
            P(("dp", "fsdp")),
            P(("dp", "fsdp")),
        ),
        out_specs=(
            P(("dp", "fsdp"), None),
            P(("dp", "fsdp"), None),
            P(("dp", "fsdp"), None),
            P(("dp", "fsdp"), None),
            P(("dp", "fsdp"), None),
            P(("dp", "fsdp"), None),
            P(("dp", "fsdp")),
            P(("dp", "fsdp")),
            P(("dp", "fsdp")),
            P(("dp", "fsdp")),
            P(("dp", "fsdp")),
            P(("dp", "fsdp"), None),
            P(("dp", "fsdp")),
            P(("dp", "fsdp"), None),
            P(("dp", "fsdp")),
            P(("dp", "fsdp")),
            P(("dp", "fsdp")),
        ),
        check_vma=False,
    )
```

time: 1660 us -> 888 us (0.53)
  waiting for transfers between devices: 916 us -> 499 us
  matrix products: 407 us -> 148 us
  blocking collectives: 111 us -> 0 us
  Pallas kernels: 0 us -> 104 us
  other arithmetic: 114 us -> 30.3 us
    unnamed x15 -> x4, waiting for transfers between devices: 253 us -> 0.57 us
    dot_general x18 -> x7, matrix products: 249 us -> 29.6 us  [the longest x3 16 us: local(): jnp.einsum('sd,se->de', tokens, g, preferred_element_type=f32).astype(bf16)]
    reduce_scatter x3 -> x2, waiting for transfers between devices: 543 us -> 377 us  [scatter_sum(): lax.psum_scatter(packed, ('dp', 'fsdp'), scatter_dimension=0, tiled=True)[0]]
    pallas_call x0 -> x2, Pallas kernels: none -> 104 us  [the longest x1 52.7 us: attend_back(): pl.pallas_call(attend_back_kernel, grid_spec=pltpu.PrefetchScalarGridSpec...]
    unnamed x2 -> x0, blocking collectives: 82 us -> none
    convert_element_type x9 -> x3, other arithmetic: 61.1 us -> 2.83 us  [the longest x1 1.2 us: local(): rest_sums.astype(f32)[None]]
    dot_general x1, matrix products: 47.4 us -> 15.5 us  [local(): jnp.dot(hidden_low, inner_full, preferred_element_type=f32)]
    reduce_sum x2 -> x0, other arithmetic: 30.1 us -> none  [attend_block(): jnp.sum(jnp.exp(scores - largest), axis=-1, keepdims=True)]
  transfers between devices with their start and end apart: 12 -> 4, of which waited for: 9 -> 4; matrix products, arithmetic and copies ran while one was open for 17% -> 6% of each run, Pallas kernels for 0% -> 6%
where the time goes in v1:
time: 888 us; the launch traced here: 883 us
  waiting for transfers between devices  499 us (56%)
  matrix products  148 us (17%)
  Pallas kernels  104 us (12%)
  local copies, waits for them, and re-layouts  86.7 us (10%)
  other arithmetic  30.3 us (3%)
  between operations  14.9 us (2%)
    reduce_scatter x2, waiting for transfers between devices, scatter_sum(): lax.psum_scatter(packed, ('dp', 'fsdp'), scatter_dimension=0, tiled=True)[0]  377 us
    all_gather x2, waiting for transfers between devices, gather(): return lax.all_gather(packed[0], ('dp', 'fsdp'), axis=0, tiled=False)  121 us
    unnamed x136, local copies, waits for them, and re-layouts  59.3 us
    pallas_call x1, Pallas kernels, attend_back(): pl.pallas_call(attend_back_kernel, grid_spec=pltpu.PrefetchScalarGridSpec...  52.7 us
    pallas_call x1, Pallas kernels, attend(): pl.pallas_call(attend_kernel, grid_spec=pltpu.PrefetchScalarGridSpec(num_...  51.2 us
    dot_general x1, matrix products, local(): jnp.dot(activated, outer_full, preferred_element_type=f32)  25.7 us
    dot_general x1, matrix products, local(): jnp.einsum('sf,df->sd', inner_low, inner_full, preferred_element_type=f32)  19 us
    dot_general x1, matrix products, local(): jnp.einsum('sd,fd->sf', outer_low, outer_full, preferred_element_type=f32)  18.3 us
  transfers between devices with their start and end apart: 4, of which 4 were waited for; matrix products, arithmetic and copies ran while one was open for 6% of the time, Pallas kernels for 6%

profile of v1, /device:TPU:14, one launch (start us, length us, event | category | flops | bytes accessed | tf_op | source)
XLA Modules:
  0.0 883.1 jit_solution(13266558222229087040)
XLA Ops:
  16.0 69.2 %all-gather.3.cloned.1.call-done = bf16[32,112,1024]{2,1,0:T(8,128)(2,1)} async-done(((bf16[1,112,1024]{2,1,0:T(8,128)(2,1)}), bf16[32,112,1024]{2,1,0:T(8,128)(2,1)}) %all-gather.3.cloned.1.call-update) | async-done | bytes 7340048 | tf_op jit(solution)/shard_map/all_gather | solution.py:270
  89.3 4.0 copy.59
  97.3 4.4 fusion.49
  109.4 51.2 %attend.1 = (bf16[1024,1024]{1,0:T(8,128)(2,1)S(1)}, f32[8,2,1024]{2,1,0:T(2,128)S(1)}) custom-call(s32[4]{0:T(128)S(1)} %get-tuple-element.103.low_ref, s32[4]{0:T(128)S(1)} %get-tuple-element.102.high_ref, bf16[1024,1024]{1,0:T(8,128)(2,1)S(1)} %fusion.10.q_ref, bf16[1024,1024]{1,0:T(8,128)(2,1)S(1)} %convert_bitcast_fusion.k_ref, ...), custom_call_target="tpu_custom_call" | custom-call | flops 4294967296 | bytes 8388608 | tf_op jit(solution)/shard_map/attend/pallas_call | solution.py:176
  162.8 51.9 %all-gather.5.cloned.1.call-done = bf16[32,304,1024]{2,1,0:T(8,128)(2,1)} async-done(((bf16[1,304,1024]{2,1,0:T(8,128)(2,1)}), bf16[32,304,1024]{2,1,0:T(8,128)(2,1)}) %all-gather.5.cloned.1.call-update) | async-done | bytes 19922960 | tf_op jit(solution)/shard_map/all_gather | solution.py:270
  217.2 5.1 fusion.48
  228.9 15.5 %multiply_convert_fusion = (bf16[1024,4096]{1,0:T(8,128)(2,1)}, f32[1024,4096]{1,0:T(8,128)}) fusion(f32[4096]{0:T(1024)S(1)} %fusion.39, bf16[1024,1024]{0,1:T(8,128)(2,1)S(1)} %fusion.9, bf16[1024,1024]{1,0:T(8,128)(2,1)S(1)} %bitcast.163, bf16[1024,1024]{1,0:T(8,128)(2,1)S(1)} %bitcast.165, bf16[1024,1024]{1,0:T(8,128)(2,1)S(1)} %bitcast.167, ...), kind=kOutput, calls=%fused_computation.7 | convolution fusion | flops 8648654848 | bytes 35667968 | tf_op jit(solution)/shard_map/dot_general | solution.py:346
  244.4 8.3 slice.208
  252.7 25.7 %fusion.51 = (f32[1024]{0:T(1024)S(1)}, f32[1024,1024]{0,1:T(8,128)}) fusion(f32[1024]{0:T(1024)S(1)} %reshape.529, bf16[1024,4096]{1,0:T(8,128)(2,1)} %get-tuple-element.143, bf16[4096,1024]{1,0:T(8,128)(2,1)} %bitcast.147, f32[1024]{0:T(1024)S(1)} %reshape.527, f32[1024]{0:T(1024)S(1)} %reshape.526, f32[1024]{0:T(1024)S(1)} %add_rsqrt_fusion.1, ...), kind=kOutput, calls=%fused_computation.142 | convolution fusion | flops 8597273600 | bytes 25190400 | tf_op jit(solution)/shard_map/dot_general | solution.py:348
  281.8 3.4 multiply_reduce_fusion
  287.4 11.3 %convolution_convert_fusion = bf16[4096,1024]{1,0:T(8,128)(2,1)} fusion(bf16[1024,4096]{1,0:T(8,128)(2,1)S(1)} %bitcast.204, bf16[1024,1024]{0,1:T(8,128)(2,1)S(1)} %get-tuple-element.105), kind=kOutput, calls=%fused_computation.10 | convolution fusion | flops 8594128896 | bytes 18874368 | tf_op jit(solution)/shard_map/sf,sd->fd/dot_general | solution.py:356
  298.7 18.3 %fusion.52 = (bf16[4096]{0:T(1024)(128)(2,1)S(1)}, bf16[1024,4096]{1,0:T(8,128)(2,1)}) fusion(f32[1024,4096]{1,0:T(8,128)} %get-tuple-element.144, f32[4096]{0:T(1024)S(1)} %fusion.39, bf16[1024,1024]{0,1:T(8,128)(2,1)S(1)} %get-tuple-element.105, bf16[4096,1024]{1,0:T(8,128)(2,1)S(1)} %bitcast.150), kind=kOutput, calls=%fused_computation.143 | convolution fusion | flops 8640262144 | bytes 35676160 | tf_op jit(solution)/shard_map/sd,fd->sf/dot_general | solution.py:358
  317.0 19.0 %multiply_reduce_fusion.1 = (bf16[1024]{0:T(1024)(128)(2,1)S(1)}, f32[1024]{0:T(1024)S(1)}, f32[1024]{0:T(1024)S(1)}, bf16[1024]{0:T(1024)(128)(2,1)S(1)}, f32[1024,1024]{0,1:T(8,128)}) fusion(f32[1024,1024]{0,1:T(8,128)} %copy-done.21, f32[1024]{0:T(1024)S(1)} %add_rsqrt_fusion.1, f32[1024]{0:T(1024)S(1)} %broadcast_multiply_fusion.5, ...), kind=kOutput, calls=%fused_computation.14 | convolution fusion | flops 8643407872 | bytes 31506432 | tf_op jit(solution)/shard_map/sf,df->sd/dot_general | solution.py:365
  336.1 5.0 convert_reduce_fusion.1
  341.1 3.7 convolution_convert_fusion.4.g_ref
  344.9 3.8 convolution_convert_fusion.5
  351.0 3.8 fusion.28
  354.8 3.7 fusion.25
  358.4 3.9 fusion.22
  367.3 6.7 copy-done.25
  374.0 8.3 constant_dynamic-update-slice_fusion.2
  391.4 52.7 %attend_back.1 = (bf16[1024,1024]{1,0:T(8,128)(2,1)S(1)}, bf16[1024,1024]{1,0:T(8,128)(2,1)S(1)}, bf16[1024,1024]{1,0:T(8,128)(2,1)S(1)}) custom-call(s32[4]{0:T(128)S(1)} %copy-done.8, s32[4]{0:T(128)S(1)} %copy-done.6, bf16[1024,1024]{1,0:T(8,128)(2,1)S(1)} %copy-done.18, bf16[1024,1024]{1,0:T(8,128)(2,1)S(1)} %copy-done.12, ...), custom_call_target="tpu_custom_call" | custom-call | flops 10737418240 | bytes 16777216 | tf_op jit(solution)/shard_map/attend_back/pallas_call | solution.py:209
  448.8 5.9 convolution_convert_fusion.3
  455.1 5.3 convolution_convert_fusion.1
  461.2 4.8 convolution_convert_fusion.2
  466.0 3.7 pad_maximum_fusion.1
  470.3 4.2 copy.69
  474.5 4.7 fusion.53
  482.1 4.6 add_add_fusion
  486.7 5.3 copy.70
  492.0 131.7 %reduce-scatter.3.cloned.1.call-done = bf16[1,112,1024]{2,1,0:T(8,128)(2,1)} async-done(((bf16[32,112,1024]{2,1,0:T(8,128)(2,1)}), bf16[1,112,1024]{2,1,0:T(8,128)(2,1)}) %reduce-scatter.3.cloned.1.call-update) | async-done | bytes 229392 | tf_op jit(solution)/shard_map/reduce_scatter | solution.py:274
  626.1 245.3 %reduce-scatter.5.cloned.1.call-done = bf16[1,304,1024]{2,1,0:T(8,128)(2,1)} async-done(((bf16[32,304,1024]{2,1,0:T(8,128)(2,1)}), bf16[1,304,1024]{2,1,0:T(8,128)(2,1)}) %reduce-scatter.5.cloned.1.call-update) | async-done | bytes 622608 | tf_op jit(solution)/shard_map/reduce_scatter | solution.py:274
  (215 shorter events, 74.0 us)
Async XLA Ops:
  7.2 79.6 %copy-start.39 = (bf16[1024,1024]{1,0:T(8,128)(2,1)S(1)}, bf16[1024,1024]{1,0:T(8,128)(2,1)}, u32[]{:S(2)}) copy-start(bf16[1024,1024]{1,0:T(8,128)(2,1)} %param.20) | copy-start | bytes 6291460
  7.2 78.0 %all-gather.3.cloned.1.call-start = ((), (), s32[]{:S(2)}) async-start(), calls=%async_computation.2 | async-start | bytes 7569408 | tf_op jit(solution)/shard_map/all_gather | solution.py:270
  9.8 204.9 %all-gather.5.cloned.1.call-start = ((), (), s32[]{:S(2)}) async-start(), calls=%async_computation.3 | async-start | bytes 20545536 | tf_op jit(solution)/shard_map/all_gather | solution.py:270
  16.0 69.2 %copy-start.49 = (bf16[1,304,1024]{2,1,0:T(8,128)(2,1)}, bf16[1,304,1024]{2,1,0:T(8,128)(2,1)S(1)}, u32[]{:S(2)}) copy-start(bf16[1,304,1024]{2,1,0:T(8,128)(2,1)S(1)} %constant_dynamic-update-slice_fusion) | copy-start | bytes 1867780
  85.2 538.5 %reduce-scatter.3.cloned.1.call-start = ((), (), s32[]{:S(2)}) async-start(), calls=%async_computation.4 | async-start | bytes 7569408 | tf_op jit(solution)/shard_map/reduce_scatter | solution.py:274
  89.3 7.1 slice-start.2
  95.8 13.2 %copy-start.5 = (s32[4]{0:T(128)}, s32[4]{0:T(128)S(1)}, u32[]{:S(2)}) copy-start(s32[4]{0:T(128)S(1)} %get-tuple-element.102.high_ref) | copy-start | bytes 52
  95.8 13.2 %copy-start.7 = (s32[4]{0:T(128)}, s32[4]{0:T(128)S(1)}, u32[]{:S(2)}) copy-start(s32[4]{0:T(128)S(1)} %get-tuple-element.103.low_ref) | copy-start | bytes 52
  104.1 5.0 copy-start.11
  162.8 59.6 %copy-start.13 = (bf16[1024,1024]{1,0:T(8,128)(2,1)}, bf16[1024,1024]{1,0:T(8,128)(2,1)S(1)}, u32[]{:S(2)}) copy-start(bf16[1024,1024]{1,0:T(8,128)(2,1)S(1)} %get-tuple-element.31.o_ref) | copy-start | bytes 6291460
  217.2 5.2 copy-start.41
  222.3 5.3 copy-start.33
  222.3 5.3 copy-start.34
  222.3 5.3 copy-start.35
  222.3 5.3 copy-start.36
  252.7 28.5 %copy-start.26 = (bf16[1024,1024]{0,1:T(8,128)(2,1)S(1)}, bf16[1024,1024]{0,1:T(8,128)(2,1)}, u32[]{:S(2)}) copy-start(bf16[1024,1024]{0,1:T(8,128)(2,1)} %copy.64) | copy-start | bytes 6291460
  281.8 5.6 slice-start.5
  285.2 13.5 %slice-start = ((s8[8388608]{0:T(1024)(128)(4,1)}), s8[4194304]{0:T(1024)(128)(4,1)S(1)}, s32[]{:S(2)}) async-start(s8[8388608]{0:T(1024)(128)(4,1)} %bitcast.148), calls=%async_computation.6 | async-start | bytes 8388608
  287.4 11.3 %slice-start.1 = ((s8[8388608]{0:T(1024)(128)(4,1)}), s8[4194304]{0:T(1024)(128)(4,1)S(1)}, s32[]{:S(2)}) async-start(s8[8388608]{0:T(1024)(128)(4,1)} %bitcast.148), calls=%async_computation.7 | async-start | bytes 8388608
  336.1 5.0 copy-start.30
  336.1 12.6 %slice-start.3 = ((s8[8388608]{0:T(1024)(128)(4,1)}), s8[4194304]{0:T(1024)(128)(4,1)S(1)}, s32[]{:S(2)}) async-start(s8[8388608]{0:T(1024)(128)(4,1)} %bitcast.201), calls=%async_computation.9 | async-start | bytes 8388608
  341.1 7.5 slice-start.4
  367.3 6.7 copy-start.25
  374.0 9.4 %copy-start.2 = (s32[1024,128]{1,0:T(8,128)S(1)}, s32[1024,128]{1,0:T(8,128)}, u32[]{:S(2)}) copy-start(s32[1024,128]{1,0:T(8,128)} %copy-done.1) | copy-start | bytes 1572868
  374.0 9.4 %copy-start.4 = (s32[8,1024]{1,0:T(8,128)S(1)}, s32[8,1024]{1,0:T(8,128)}, u32[]{:S(2)}) copy-start(s32[8,1024]{1,0:T(8,128)} %copy-done.3) | copy-start | bytes 98308
  374.0 9.4 %copy-start.6 = (s32[4]{0:T(128)S(1)}, s32[4]{0:T(128)}, u32[]{:S(2)}) copy-start(s32[4]{0:T(128)} %copy-done.5) | copy-start | bytes 52
  374.0 9.4 %copy-start.8 = (s32[4]{0:T(128)S(1)}, s32[4]{0:T(128)}, u32[]{:S(2)}) copy-start(s32[4]{0:T(128)} %copy-done.7) | copy-start | bytes 52
  461.2 4.8 copy-start.37
  461.2 4.8 copy-start.38
  469.7 401.7 %reduce-scatter.5.cloned.1.call-start = ((), (), s32[]{:S(2)}) async-start(), calls=%async_computation.5 | async-start | bytes 20545536 | tf_op jit(solution)/shard_map/reduce_scatter | solution.py:274
  474.4 4.8 copy-start.10
  474.5 4.8 copy-start.47
  (29 other events, 66.1 us)
Sparse Core Ops, SparseCore 0:
  11.4 73.6 all-gather.2
  88.0 126.6 all-gather.4
  469.8 153.8 reduce-scatter.2
  625.9 245.4 reduce-scatter.4
